TPU v7x, 512 devices: a whole 4x8x8 slice. The times are simulated.
512 devices in a mesh: blk: 256 (over y, z_hi, x, core), rep: 2 (over z_lo).
Axes of the slice: x: 4, y: 8, z: 8 (z_hi: 4, z_lo: 2; z = z_hi * 2 + z_lo), core: 2. Of those that a mesh axis runs over, the one named last changes fastest.
Arguments:
- positions: float32 [3, 262144], P(None, ('blk', 'rep')), may hold values from -5 to 5
- velocities: float32 [3, 262144], P(None, ('blk', 'rep')), may hold values from -5 to 5
- masses: float32 [262144], P(('blk', 'rep')), may hold values from 0.2 to 2
Outputs:
- star_accel: float32 [3, 262144], P(None, ('blk', 'rep'))
- star_jerk: float32 [3, 262144], P(None, ('blk', 'rep'))
All inputs are finite; a program needn't handle non-finite values.
Results may differ from a plain program's by a relative error of at most 0.00015.
Values sent between devices are 32-bit elements; how exact they have to be, the bound alone decides.
A program may use at most 64 MiB of HBM per device.

v0:
```python
import jax
import jax.numpy as jnp
from jax import lax
from jax.sharding import PartitionSpec as P

BLOCK = 1024
STEPS = 4


SOFTENING_SQ = 0.01


def shifted(value, axis, by):
    devices = lax.axis_size(axis)
    return lax.ppermute(value, axis, [(i, (i + by) % devices) for i in range(devices)])


def pair_tile(targets, sources):
    coupling = 1.0 / BLOCK
    offset = sources[0:3, None, :] - targets[0:3, :, None]
    closing = sources[3:6, None, :] - targets[3:6, :, None]
    radius_sq = offset[0] * offset[0] + offset[1] * offset[1] + offset[2] * offset[2] + SOFTENING_SQ
    inverse = lax.rsqrt(radius_sq)
    inverse_cube = inverse * inverse * inverse * coupling
    factor = (
        3.0
        * (offset[0] * closing[0] + offset[1] * closing[1] + offset[2] * closing[2])
        * inverse
        * inverse
    )
    pull_term = inverse_cube[None] * offset
    jolt_term = inverse_cube[None] * (closing - factor[None] * offset)
    pair_terms = jnp.concatenate([pull_term, jolt_term], 0)
    own_part = jnp.sum(pair_terms * sources[6][None, None, :], 2)
    reaction = -jnp.sum(pair_terms * targets[6][None, :, None], 1)
    return (own_part, reaction)


def block_field(targets, sources):
    row_total = targets.shape[1]
    piece_rows = min(256, row_total)
    pieces = targets.reshape(7, row_total // piece_rows, piece_rows).transpose(1, 0, 2)
    own_part, reaction = lax.map(lambda target_rows: pair_tile(target_rows, sources), pieces)
    own_part = own_part.transpose(1, 0, 2).reshape(6, row_total)
    return (own_part, jnp.sum(reaction, 0))


def settle(partial_value):
    return lax.psum_scatter(partial_value, "rep", scatter_dimension=1, tiled=True)


def send_home(carried):
    for hop_index in range(STEPS):
        carried = shifted(carried, "blk", -1)
    return carried


def body(positions, velocities, masses):
    own_half = jnp.concatenate([positions, velocities, masses[None]], 0)
    own_block = lax.all_gather(own_half, "rep", axis=1, tiled=True)
    own_sum = block_field(own_half, own_block)[0]
    visitor = shifted(own_block, "blk", 1)
    gained, carried = block_field(own_half, visitor)
    own_sum = own_sum + gained
    for hop_index in range(1, STEPS):
        visitor, carried = shifted((visitor, carried), "blk", 1)
        gained, reaction = block_field(own_half, visitor)
        own_sum = own_sum + gained
        carried = carried + reaction
    carried = settle(carried)
    returned = send_home(carried)
    summed = own_sum + returned
    return (summed[0:3], summed[3:6])


def solution(mesh):
    return jax.shard_map(
        body,
        mesh=mesh,
        in_specs=(P(None, ("blk", "rep")), P(None, ("blk", "rep")), P(("blk", "rep"))),
        out_specs=(P(None, ("blk", "rep")), P(None, ("blk", "rep"))),
        check_vma=False,
    )
```

profile of v0, /device:TPU:64, one launch (start us, length us, event | category | flops | bytes accessed | tf_op | source)
XLA Modules:
  0.0 148.8 jit_solution(925127728306072839)
XLA Ops:
  8.0 7.4 %all_gather.3 = f32[7,1024]{1,0:T(8,128)S(1)} all-gather(f32[7,512]{1,0:T(8,128)S(1)} %pad_maximum_fusion.4), channel_id=1, replica_groups=mesh['blk'=256,'rep'=2] {'rep'}, dimensions={1}, use_global_device_ids=true | all-gather | bytes 43008 | tf_op jit(solution)/shard_map/all_gather | solution.py:60
  15.4 1.9 %collective-permute-start = (f32[7,1024]{1,0:T(8,128)S(1)}, f32[7,1024]{1,0:T(8,128)}, u32[]{:S(2)}, u32[]{:S(2)}) collective-permute-start(f32[7,1024]{1,0:T(8,128)S(1)} %all_gather.3), channel_id=1, source_target_pairs={{0,2},{2,4},{4,6},{6,8},{8,10},{10,12},{12,14},{14,16},{16,18},{18... | collective-permute-start | bytes 86024 | tf_op jit(solution)/shard_map/ppermute | solution.py:15
  18.0 9.5 %collective-permute-done = f32[7,1024]{1,0:T(8,128)} collective-permute-done((f32[7,1024]{1,0:T(8,128)S(1)}, f32[7,1024]{1,0:T(8,128)}, u32[]{:S(2)}, u32[]{:S(2)}) %collective-permute-start) | collective-permute-done | bytes 28704 | tf_op jit(solution)/shard_map/ppermute | solution.py:15
  27.5 1.9 %collective-permute-start.1 = (f32[7,1024]{1,0:T(8,128)}, f32[7,1024]{1,0:T(8,128)}, u32[]{:S(2)}, u32[]{:S(2)}) collective-permute-start(f32[7,1024]{1,0:T(8,128)} %collective-permute-done), channel_id=1, source_target_pairs={{0,2},{2,4},{4,6},{6,8},{8,10},{10,12},{12,14},{14,16},{16,18},{18... | collective-permute-start | bytes 86024 | tf_op jit(solution)/shard_map/ppermute | solution.py:15
  29.4 10.1 %while.59 = (s32[]{:T(128)}, f32[2,6,256]{2,1,0:T(8,128)S(1)}, f32[2,6,1024]{2,1,0:T(8,128)S(1)}, f32[7,1024]{1,0:T(8,128)}, f32[2,7,256]{2,1,0:T(8,128)S(1)}, /*index=5*/s32[]{:T(128)}, s32[]{:T(128)}, s32[]{}, s32[]{}) while((s32[]{:T(128)}, f32[2,6,256]{2,1,0:T(8,128)S(1)}, f32[2,6,1024]{2,1,0:T(8,128)S(1)}, f32[7,1024]{1,0:T(8,128)}, ...), condition=%wide.region_6.7_spmd, body=%wide.region_3.6_spmd.sunk | while | flops 18610692 | bytes 29611156 | solution.py:43
  33.2 1.2 multiply_reduce_fusion.12
  37.4 0.9 subtract_multiply_fusion.16
  38.3 1.2 multiply_reduce_fusion.12
  39.6 1.9 %collective-permute-start.4 = (f32[6,1024]{1,0:T(8,128)S(1)}, f32[6,1024]{1,0:T(8,128)S(1)}, u32[]{:S(2)}, u32[]{:S(2)}) collective-permute-start(f32[6,1024]{1,0:T(8,128)S(1)} %reduce_sum.117), channel_id=1, source_target_pairs={{0,2},{2,4},{4,6},{6,8},{8,10},{10,12},{12,14},{14,16},{16,18},{18... | collective-permute-start | bytes 73736 | tf_op jit(solution)/shard_map/ppermute | solution.py:15
  41.5 1.9 %collective-permute-start.2 = (f32[7,1024]{1,0:T(8,128)}, f32[7,1024]{1,0:T(8,128)}, u32[]{:S(2)}, u32[]{:S(2)}) collective-permute-start(f32[7,1024]{1,0:T(8,128)} %collective-permute-done.1), channel_id=1, source_target_pairs={{0,2},{2,4},{4,6},{6,8},{8,10},{10,12},{12,14},{14,16},{16,18},{18... | collective-permute-start | bytes 86024 | tf_op jit(solution)/shard_map/ppermute | solution.py:15
  43.5 10.1 %while.60 = (s32[]{:T(128)}, f32[2,6,256]{2,1,0:T(8,128)S(1)}, f32[2,6,1024]{2,1,0:T(8,128)S(1)}, f32[7,1024]{1,0:T(8,128)}, f32[2,7,256]{2,1,0:T(8,128)S(1)}, /*index=5*/s32[]{:T(128)}, s32[]{:T(128)}, s32[]{}, s32[]{}) while((s32[]{:T(128)}, f32[2,6,256]{2,1,0:T(8,128)S(1)}, f32[2,6,1024]{2,1,0:T(8,128)S(1)}, f32[7,1024]{1,0:T(8,128)}, ...), condition=%wide.region_10.11_spmd, body=%wide.region_7.10_spmd.sunk | while | flops 18610692 | bytes 29611156 | solution.py:43
  47.3 1.2 multiply_reduce_fusion.13
  52.3 1.2 multiply_reduce_fusion.13
  53.6 1.9 %collective-permute-start.5 = (f32[6,1024]{1,0:T(8,128)S(1)}, f32[6,1024]{1,0:T(8,128)S(1)}, u32[]{:S(2)}, u32[]{:S(2)}) collective-permute-start(f32[6,1024]{1,0:T(8,128)S(1)} %add.173), channel_id=1, source_target_pairs={{0,2},{2,4},{4,6},{6,8},{8,10},{10,12},{12,14},{14,16},{16,18},{18... | collective-permute-start | bytes 73736 | tf_op jit(solution)/shard_map/ppermute | solution.py:15
  55.6 1.9 %collective-permute-start.3 = (f32[7,1024]{1,0:T(8,128)}, f32[7,1024]{1,0:T(8,128)S(1)}, u32[]{:S(2)}, u32[]{:S(2)}) collective-permute-start(f32[7,1024]{1,0:T(8,128)} %collective-permute-done.2), channel_id=1, source_target_pairs={{0,2},{2,4},{4,6},{6,8},{8,10},{10,12},{12,14},{14,16},{16,18},{18... | collective-permute-start | bytes 86024 | tf_op jit(solution)/shard_map/ppermute | solution.py:15
  57.5 10.1 %while.61 = (s32[]{:T(128)}, f32[2,6,256]{2,1,0:T(8,128)S(1)}, f32[2,6,1024]{2,1,0:T(8,128)S(1)}, f32[7,1024]{1,0:T(8,128)}, f32[2,7,256]{2,1,0:T(8,128)S(1)}, /*index=5*/s32[]{:T(128)}, s32[]{:T(128)}, s32[]{}, s32[]{}) while((s32[]{:T(128)}, f32[2,6,256]{2,1,0:T(8,128)S(1)}, f32[2,6,1024]{2,1,0:T(8,128)S(1)}, f32[7,1024]{1,0:T(8,128)}, ...), condition=%wide.region_14.15_spmd, body=%wide.region_11.14_spmd.sunk | while | flops 18610692 | bytes 29611156 | solution.py:43
  61.3 1.2 multiply_reduce_fusion.14
  66.3 1.2 multiply_reduce_fusion.14
  67.6 2.1 %collective-permute-start.6 = (f32[6,1024]{1,0:T(8,128)S(1)}, f32[6,1024]{1,0:T(8,128)S(1)}, u32[]{:S(2)}, u32[]{:S(2)}) collective-permute-start(f32[6,1024]{1,0:T(8,128)S(1)} %add.174), channel_id=1, source_target_pairs={{0,2},{2,4},{4,6},{6,8},{8,10},{10,12},{12,14},{14,16},{16,18},{18... | collective-permute-start | bytes 73736 | tf_op jit(solution)/shard_map/ppermute | solution.py:15
  69.8 7.0 %while.62 = (s32[]{:T(128)}, f32[2,6,256]{2,1,0:T(8,128)S(1)}, f32[2,6,1024]{2,1,0:T(8,128)S(1)}, f32[7,1024]{1,0:T(8,128)S(1)}, f32[2,7,256]{2,1,0:T(8,128)S(1)}, /*index=5*/s32[]{:T(128)}, s32[]{:T(128)}, s32[]{}, s32[]{}) while((s32[]{:T(128)}, f32[2,6,256]{2,1,0:T(8,128)S(1)}, f32[2,6,1024]{2,1,0:T(8,128)S(1)}, ...), condition=%wide.region_18.19_spmd, body=%wide.region_15.0_spmd.sunk | while | flops 18610692 | bytes 29611156 | solution.py:43
  72.0 1.2 multiply_reduce_fusion.15
  75.5 1.2 multiply_reduce_fusion.15
  76.8 2.4 %collective-permute-done.6 = f32[6,1024]{1,0:T(8,128)S(1)} collective-permute-done((f32[6,1024]{1,0:T(8,128)S(1)}, f32[6,1024]{1,0:T(8,128)S(1)}, u32[]{:S(2)}, u32[]{:S(2)}) %collective-permute-start.6) | collective-permute-done | bytes 24608 | tf_op jit(solution)/shard_map/ppermute | solution.py:15
  79.8 16.8 %reduce-scatter.2.cloned.1.call-done = f32[6,512]{1,0:T(8,128)} async-done(((f32[6,1024]{1,0:T(8,128)}), f32[6,512]{1,0:T(8,128)}) %reduce-scatter.2.cloned.1.call-update) | async-done | bytes 12304 | tf_op jit(solution)/shard_map/reduce_scatter | solution.py:49
  96.6 8.9 %collective-permute-start.7 = (f32[6,512]{1,0:T(8,128)}, f32[6,512]{1,0:T(8,128)S(1)}, u32[]{:S(2)}, u32[]{:S(2)}) collective-permute-start(f32[6,512]{1,0:T(8,128)} %reduce-scatter.2.cloned.1.call-done), channel_id=1, source_target_pairs={{0,510},{2,0},{4,2},{6,4},{8,6},{10,8},{12,10},{14,12},{16,14},{18... | collective-permute-start | bytes 36872 | tf_op jit(solution)/shard_map/ppermute | solution.py:15
  105.6 1.6 %collective-permute-done.7 = f32[6,512]{1,0:T(8,128)S(1)} collective-permute-done((f32[6,512]{1,0:T(8,128)}, f32[6,512]{1,0:T(8,128)S(1)}, u32[]{:S(2)}, u32[]{:S(2)}) %collective-permute-start.7) | collective-permute-done | bytes 12320 | tf_op jit(solution)/shard_map/ppermute | solution.py:15
  107.2 9.9 %collective-permute-start.8 = (f32[6,512]{1,0:T(8,128)S(1)}, f32[6,512]{1,0:T(8,128)S(1)}, u32[]{:S(2)}, u32[]{:S(2)}) collective-permute-start(f32[6,512]{1,0:T(8,128)S(1)} %collective-permute-done.7), channel_id=1, source_target_pairs={{0,510},{2,0},{4,2},{6,4},{8,6},{10,8},{12,10},{14,12},{16,14},{18... | collective-permute-start | bytes 36872 | tf_op jit(solution)/shard_map/ppermute | solution.py:15
  117.2 1.4 collective-permute-done.8
  118.6 9.9 %collective-permute-start.9 = (f32[6,512]{1,0:T(8,128)S(1)}, f32[6,512]{1,0:T(8,128)S(1)}, u32[]{:S(2)}, u32[]{:S(2)}) collective-permute-start(f32[6,512]{1,0:T(8,128)S(1)} %collective-permute-done.8), channel_id=1, source_target_pairs={{0,510},{2,0},{4,2},{6,4},{8,6},{10,8},{12,10},{14,12},{16,14},{18... | collective-permute-start | bytes 36872 | tf_op jit(solution)/shard_map/ppermute | solution.py:15
  128.6 5.4 %while.58 = (s32[]{:T(128)}, f32[2,6,256]{2,1,0:T(8,128)S(1)}, f32[7,1024]{1,0:T(8,128)S(1)}, f32[2,7,256]{2,1,0:T(8,128)S(1)}, s32[]{:T(128)}, /*index=5*/s32[]{:T(128)}, s32[]{}) while((s32[]{:T(128)}, f32[2,6,256]{2,1,0:T(8,128)S(1)}, f32[7,1024]{1,0:T(8,128)S(1)}, f32[2,7,256]{2,1,0:T(8,128)S(1)}, s32[]{:T(128)}, /*index=5*/s32[]{:T(128)}, ...), condition=%wide.region_2.3_spmd, body=%wide.region_0.2_spmd.sunk | while | flops 15464963 | bytes 29517932 | solution.py:43
  134.0 5.9 %collective-permute-start.10 = (f32[6,512]{1,0:T(8,128)S(1)}, f32[6,512]{1,0:T(8,128)S(1)}, u32[]{:S(2)}, u32[]{:S(2)}) collective-permute-start(f32[6,512]{1,0:T(8,128)S(1)} %collective-permute-done.9), channel_id=1, source_target_pairs={{0,510},{2,0},{4,2},{6,4},{8,6},{10,8},{12,10},{14,12},{16,14},{18... | collective-permute-start | bytes 36872 | tf_op jit(solution)/shard_map/ppermute | solution.py:15
  140.0 1.4 collective-permute-done.10
  (124 shorter events, 34.2 us)
Async XLA Ops:
  7.2 89.5 %reduce-scatter.2.cloned.1.call-start = ((), (), s32[]{:S(2)}) async-start(), calls=%async_computation.1 | async-start | bytes 49152 | tf_op jit(solution)/shard_map/reduce_scatter | solution.py:49
  15.3 14.1 %copy-start = (f32[7,1024]{1,0:T(8,128)}, f32[7,1024]{1,0:T(8,128)S(1)}, u32[]{:S(2)}) copy-start(f32[7,1024]{1,0:T(8,128)S(1)} %all_gather.3) | copy-start | bytes 86020
  15.4 12.1 %collective-permute-start = (f32[7,1024]{1,0:T(8,128)S(1)}, f32[7,1024]{1,0:T(8,128)}, u32[]{:S(2)}, u32[]{:S(2)}) collective-permute-start(f32[7,1024]{1,0:T(8,128)S(1)} %all_gather.3), channel_id=1, source_target_pairs={{0,2},{2,4},{4,6},{6,8},{8,10},{10,12},{12,14},{14,16},{16,18},{18... | collective-permute-start | bytes 86024 | tf_op jit(solution)/shard_map/ppermute | solution.py:15
  27.5 14.0 %collective-permute-start.1 = (f32[7,1024]{1,0:T(8,128)}, f32[7,1024]{1,0:T(8,128)}, u32[]{:S(2)}, u32[]{:S(2)}) collective-permute-start(f32[7,1024]{1,0:T(8,128)} %collective-permute-done), channel_id=1, source_target_pairs={{0,2},{2,4},{4,6},{6,8},{8,10},{10,12},{12,14},{14,16},{16,18},{18... | collective-permute-start | bytes 86024 | tf_op jit(solution)/shard_map/ppermute | solution.py:15
  39.5 3.9 %copy-start.2 = (f32[2,6,256]{2,1,0:T(8,128)}, f32[2,6,256]{2,1,0:T(8,128)S(1)}, u32[]{:S(2)}) copy-start(f32[2,6,256]{2,1,0:T(8,128)S(1)} %get-tuple-element.137) | copy-start | bytes 36868
  39.6 14.0 %collective-permute-start.4 = (f32[6,1024]{1,0:T(8,128)S(1)}, f32[6,1024]{1,0:T(8,128)S(1)}, u32[]{:S(2)}, u32[]{:S(2)}) collective-permute-start(f32[6,1024]{1,0:T(8,128)S(1)} %reduce_sum.117), channel_id=1, source_target_pairs={{0,2},{2,4},{4,6},{6,8},{8,10},{10,12},{12,14},{14,16},{16,18},{18... | collective-permute-start | bytes 73736 | tf_op jit(solution)/shard_map/ppermute | solution.py:15
  41.5 14.0 %collective-permute-start.2 = (f32[7,1024]{1,0:T(8,128)}, f32[7,1024]{1,0:T(8,128)}, u32[]{:S(2)}, u32[]{:S(2)}) collective-permute-start(f32[7,1024]{1,0:T(8,128)} %collective-permute-done.1), channel_id=1, source_target_pairs={{0,2},{2,4},{4,6},{6,8},{8,10},{10,12},{12,14},{14,16},{16,18},{18... | collective-permute-start | bytes 86024 | tf_op jit(solution)/shard_map/ppermute | solution.py:15
  53.6 14.0 %collective-permute-start.5 = (f32[6,1024]{1,0:T(8,128)S(1)}, f32[6,1024]{1,0:T(8,128)S(1)}, u32[]{:S(2)}, u32[]{:S(2)}) collective-permute-start(f32[6,1024]{1,0:T(8,128)S(1)} %add.173), channel_id=1, source_target_pairs={{0,2},{2,4},{4,6},{6,8},{8,10},{10,12},{12,14},{14,16},{16,18},{18... | collective-permute-start | bytes 73736 | tf_op jit(solution)/shard_map/ppermute | solution.py:15
  55.6 14.2 %collective-permute-start.3 = (f32[7,1024]{1,0:T(8,128)}, f32[7,1024]{1,0:T(8,128)S(1)}, u32[]{:S(2)}, u32[]{:S(2)}) collective-permute-start(f32[7,1024]{1,0:T(8,128)} %collective-permute-done.2), channel_id=1, source_target_pairs={{0,2},{2,4},{4,6},{6,8},{8,10},{10,12},{12,14},{14,16},{16,18},{18... | collective-permute-start | bytes 86024 | tf_op jit(solution)/shard_map/ppermute | solution.py:15
  67.6 11.6 %collective-permute-start.6 = (f32[6,1024]{1,0:T(8,128)S(1)}, f32[6,1024]{1,0:T(8,128)S(1)}, u32[]{:S(2)}, u32[]{:S(2)}) collective-permute-start(f32[6,1024]{1,0:T(8,128)S(1)} %add.174), channel_id=1, source_target_pairs={{0,2},{2,4},{4,6},{6,8},{8,10},{10,12},{12,14},{14,16},{16,18},{18... | collective-permute-start | bytes 73736 | tf_op jit(solution)/shard_map/ppermute | solution.py:15
  69.8 58.8 %copy-start.1 = (f32[7,1024]{1,0:T(8,128)S(1)}, f32[7,1024]{1,0:T(8,128)}, u32[]{:S(2)}) copy-start(f32[7,1024]{1,0:T(8,128)} %copy-done) | copy-start | bytes 86020
  96.6 10.6 %collective-permute-start.7 = (f32[6,512]{1,0:T(8,128)}, f32[6,512]{1,0:T(8,128)S(1)}, u32[]{:S(2)}, u32[]{:S(2)}) collective-permute-start(f32[6,512]{1,0:T(8,128)} %reduce-scatter.2.cloned.1.call-done), channel_id=1, source_target_pairs={{0,510},{2,0},{4,2},{6,4},{8,6},{10,8},{12,10},{14,12},{16,14},{18... | collective-permute-start | bytes 36872 | tf_op jit(solution)/shard_map/ppermute | solution.py:15
  107.2 11.4 %collective-permute-start.8 = (f32[6,512]{1,0:T(8,128)S(1)}, f32[6,512]{1,0:T(8,128)S(1)}, u32[]{:S(2)}, u32[]{:S(2)}) collective-permute-start(f32[6,512]{1,0:T(8,128)S(1)} %collective-permute-done.7), channel_id=1, source_target_pairs={{0,510},{2,0},{4,2},{6,4},{8,6},{10,8},{12,10},{14,12},{16,14},{18... | collective-permute-start | bytes 36872 | tf_op jit(solution)/shard_map/ppermute | solution.py:15
  118.6 15.4 %collective-permute-start.9 = (f32[6,512]{1,0:T(8,128)S(1)}, f32[6,512]{1,0:T(8,128)S(1)}, u32[]{:S(2)}, u32[]{:S(2)}) collective-permute-start(f32[6,512]{1,0:T(8,128)S(1)} %collective-permute-done.8), channel_id=1, source_target_pairs={{0,510},{2,0},{4,2},{6,4},{8,6},{10,8},{12,10},{14,12},{16,14},{18... | collective-permute-start | bytes 36872 | tf_op jit(solution)/shard_map/ppermute | solution.py:15
  128.6 11.4 %copy-start.3 = (f32[2,6,256]{2,1,0:T(8,128)S(1)}, f32[2,6,256]{2,1,0:T(8,128)}, u32[]{:S(2)}) copy-start(f32[2,6,256]{2,1,0:T(8,128)} %copy-done.2) | copy-start | bytes 36868
  134.0 7.4 %collective-permute-start.10 = (f32[6,512]{1,0:T(8,128)S(1)}, f32[6,512]{1,0:T(8,128)S(1)}, u32[]{:S(2)}, u32[]{:S(2)}) collective-permute-start(f32[6,512]{1,0:T(8,128)S(1)} %collective-permute-done.9), channel_id=1, source_target_pairs={{0,510},{2,0},{4,2},{6,4},{8,6},{10,8},{12,10},{14,12},{16,14},{18... | collective-permute-start | bytes 36872 | tf_op jit(solution)/shard_map/ppermute | solution.py:15
Sparse Core Ops, SparseCore 0:
  80.0 16.6 reduce-scatter.1
where the time goes:
time: 150 us; the launch traced here: 149 us
  starting transfers between devices  48.4 us (32%)
  other arithmetic  34.2 us (23%)
  waiting for transfers between devices  33.2 us (22%)
  between operations  14.4 us (10%)
  local copies, waits for them, and re-layouts  10.6 us (7%)
  blocking collectives  7.39 us (5%)
    ppermute x11, starting transfers between devices, shifted(): lax.ppermute(value, axis, [(i, (i + by) % devices) for i in range(devices)])  48.4 us
    reduce_scatter x1, waiting for transfers between devices, settle(): lax.psum_scatter(partial_value, 'rep', scatter_dimension=1, tiled=True)  16.8 us
    mul x20, other arithmetic, pair_tile(): pull_term = inverse_cube[None] * offset  16.5 us
    ppermute x11, waiting for transfers between devices, shifted(): lax.ppermute(value, axis, [(i, (i + by) % devices) for i in range(devices)])  16.4 us
    reduce_sum x8, other arithmetic, pair_tile(): reaction = -jnp.sum(pair_terms * targets[6][None, :, None], 1)  9.77 us
    all_gather x1, blocking collectives, body(): own_block = lax.all_gather(own_half, 'rep', axis=1, tiled=True)  7.39 us
    slice x10, local copies, waits for them, and re-layouts, pair_tile(): offset = sources[0:3, None, :] - targets[0:3, :, None]  5.09 us
    sub x10, other arithmetic, pair_tile(): closing = sources[3:6, None, :] - targets[3:6, :, None]  4.72 us
  transfers between devices with their start and end apart: 12, of which 6 were waited for; matrix products, arithmetic and copies ran while one was open for 29% of the time, Pallas kernels for 0%

commit v1 on v0

v1 whole, which is shorter than its diff:
```python
import jax
import jax.numpy as jnp
from jax import lax
from jax.experimental import pallas as pl
from jax.experimental.pallas import tpu as pltpu
from jax.sharding import PartitionSpec as P

BLOCK = 1024
STEPS = 4
SOFTENING_SQ = 0.01
PIECES = 3
BF = jnp.bfloat16
F32 = jnp.float32
MESH = pl.DeviceIdType.MESH


def as_bf16(value):
    return value.astype(BF).astype(F32)


def pieces(value, count):
    out = []
    for _ in range(count - 1):
        high = as_bf16(value)
        out.append(high)
        value = value - high
    out.append(as_bf16(value))
    return out


def on_grid(value):
    coarse = jnp.round(value * 32.0) * (1.0 / 32.0)
    rest = value - coarse
    first = as_bf16(rest)
    second = as_bf16(rest - first)
    return coarse, rest, first, second


def added(rows):
    return rows[0:1] + rows[1:2] + rows[2:3]


def products(pos, vel):
    xq, xr, x1, x2 = on_grid(pos)
    vq, vr, v1, v2 = on_grid(vel)
    q = pieces(added(xq * xq), 3)
    s = pieces(added(2.0 * xq * xr + xr * xr), 3)
    dq = pieces(added(xq * vq), 3)
    ds = pieces(added(xq * vr + xr * vq + xr * vr), 3)
    return (xq, x1, x2, vq, v1, v2), (q, s, dq, ds)


def source_rows(pos, vel):
    (xq, x1, x2, vq, v1, v2), (q, s, dq, ds) = products(pos, vel)
    ones = [jnp.ones_like(q[0])] * 3
    square = [xq] + q + ones + [xq, xq, x1, x2, x1, x1, x2] + s + ones
    dot = [xq, vq] + dq + ones + [xq, xq, x1, x2, x1, x1, x2] + [vq, vq, v1, v2, v1, v1, v2] + ds + ones
    return jnp.concatenate(square + dot, 0)


def target_rows(pos, vel):
    (xq, x1, x2, vq, v1, v2), (q, s, dq, ds) = products(pos, vel)
    ones = [jnp.ones_like(q[0])] * 3
    s = pieces(s[0] + s[1] + s[2] + SOFTENING_SQ, 3)
    a, b, c = -2.0 * xq, -2.0 * x1, -2.0 * x2
    square = [a] + ones + q + [b, c, a, a, b, c, b] + ones + s
    dot = [-vq, -xq] + ones + dq + [-v1, -v2, -vq, -vq, -v1, -v2, -v1] + [-x1, -x2, -xq, -xq, -x1, -x2, -x1] + ones + ds
    square = jnp.concatenate(square, 0)
    dot = jnp.concatenate(dot, 0)
    top = jnp.concatenate([square, jnp.zeros_like(square)], 1)
    bottom = jnp.concatenate([jnp.zeros_like(dot), dot], 1)
    return jnp.concatenate([top, bottom], 0)


def value_rows(pos, vel, mass):
    m = mass * (1.0 / BLOCK)
    zero = jnp.zeros_like(m)
    one = pieces(jnp.concatenate([m, m * pos, m * vel, zero], 0), PIECES)
    two = pieces(3.0 * jnp.concatenate([m, m * pos], 0), PIECES) + [jnp.zeros_like(pos[0:1])] * 4
    return jnp.concatenate(one, 0), jnp.concatenate(two, 0)


def kernel(blocks, features, p_ref, v_ref, m_ref, accel_ref, jerk_ref, mine, seen, feat, tgt, val1, val2, sum1, sum2, send_sem, recv_sem):
    blk = lax.axis_index("blk")
    rep = lax.axis_index("rep")
    half = p_ref.shape[1]
    slots = seen.shape[0]

    def offset(k):
        return (k // 2 + 1) * (1 - 2 * (k % 2))

    def peer(k, r):
        return (lax.rem(blk + offset(k) + blocks, blocks), r)

    barrier = pltpu.get_barrier_semaphore()
    pl.semaphore_signal(barrier, inc=1, device_id=(blk, 1 - rep), device_id_type=MESH)
    for k in range(2 * STEPS):
        for r in range(2):
            pl.semaphore_signal(barrier, inc=1, device_id=peer(k, r), device_id_type=MESH)

    mine[0:3] = p_ref[...]
    mine[3:6] = v_ref[...]
    mine[6:7] = m_ref[...]
    mine[7:8] = jnp.zeros((1, half), F32)
    sum1[...] = jnp.zeros_like(sum1)
    sum2[...] = jnp.zeros_like(sum2)

    def prepare(stars, into):
        feat[into] = source_rows(stars[0:3], stars[3:6]).T.astype(BF)
        one, two = value_rows(stars[0:3], stars[3:6], stars[6:7])
        val1[into] = one.astype(BF)
        val2[into] = two.astype(BF)

    def work(at):
        both = jnp.dot(feat[at], tgt[...], preferred_element_type=F32)
        inverse = lax.rsqrt(both[:, :half])
        inverse_sq = inverse * inverse
        w = inverse * inverse_sq
        w2 = w * (both[:, half:] * inverse_sq)
        high = w.astype(BF)
        low = (w - high.astype(F32)).astype(BF)
        high2 = w2.astype(BF)
        low2 = (w2 - high2.astype(F32)).astype(BF)
        one = val1[at]
        two = val2[at]
        sum1[...] += jnp.dot(one, high, preferred_element_type=F32) + jnp.dot(one, low, preferred_element_type=F32)
        sum2[...] += jnp.dot(two, high2, preferred_element_type=F32) + jnp.dot(two, low2, preferred_element_type=F32)

    def copy(src, slot, device, sent):
        return pltpu.make_async_remote_copy(
            src_ref=src,
            dst_ref=seen.at[slot],
            send_sem=send_sem.at[sent],
            recv_sem=recv_sem.at[slot],
            device_id=device,
            device_id_type=MESH,
        )

    own = mine[...]
    tgt[...] = target_rows(own[0:3], own[3:6]).astype(BF)
    prepare(own, 0)

    pl.semaphore_wait(barrier, slots - 1)
    copies = [copy(mine, 1, (blk, 1 - rep), 1)]
    for k in range(2 * STEPS):
        for r in range(2):
            copies.append(copy(mine, 2 + 2 * (k ^ 1) + rep, peer(k, r), 2 + 2 * k + r))
    for one in copies:
        one.start()

    work(0)

    def arrive(slot):
        copy(mine, slot, (blk, 1 - rep), slot).wait_recv()
        prepare(seen[slot], lax.rem(slot, 2))

    arrive(1)

    def step(slot, _):
        arrive(slot + 1)
        work(lax.rem(slot, 2))
        return 0

    lax.fori_loop(1, slots - 1, step, 0)
    work((slots - 1) % 2)

    one = sum1[0:8] + sum1[8:16] + sum1[16:24]
    two = sum2[0:4] + sum2[4:8] + sum2[8:12]
    pos, vel = own[0:3], own[3:6]
    accel_ref[...] = one[1:4] - pos * one[0:1]
    jerk_ref[...] = (one[4:7] - vel * one[0:1]) - (two[1:4] - pos * two[0:1])
    for one in copies:
        one.wait_send()


def body(positions, velocities, masses):
    half = positions.shape[1]
    blocks = lax.axis_size("blk")
    slots = 2 * (2 * STEPS + 1)
    features = 96
    vmem = pl.BlockSpec(memory_space=pltpu.VMEM)
    out = jax.ShapeDtypeStruct((3, half), F32)

    def run(*refs):
        kernel(blocks, features, *refs)

    return pl.pallas_call(
        run,
        out_shape=(out, out),
        in_specs=[vmem] * 3,
        out_specs=(vmem, vmem),
        scratch_shapes=[
            pltpu.VMEM((8, half), F32),
            pltpu.VMEM((slots, 8, half), F32),
            pltpu.VMEM((2, half, features), BF),
            pltpu.VMEM((features, 2 * half), BF),
            pltpu.VMEM((2, 8 * PIECES, half), BF),
            pltpu.VMEM((2, 16, half), BF),
            pltpu.VMEM((8 * PIECES, half), F32),
            pltpu.VMEM((16, half), F32),
            pltpu.SemaphoreType.DMA((slots,)),
            pltpu.SemaphoreType.DMA((slots,)),
        ],
        compiler_params=pltpu.CompilerParams(collective_id=0, has_side_effects=True, vmem_limit_bytes=48 << 20),
    )(positions, velocities, masses[None])


def solution(mesh):
    return jax.shard_map(
        body,
        mesh=mesh,
        in_specs=(P(None, ("blk", "rep")), P(None, ("blk", "rep")), P(("blk", "rep"))),
        out_specs=(P(None, ("blk", "rep")), P(None, ("blk", "rep"))),
        check_vma=False,
    )
```

time: 150 us -> 39.9 us (0.27)
  the two profiles are of different devices: /device:TPU:64 before, /device:TPU:1 now
where the time goes in v1:
time: 39.9 us; the launch traced here: 39.7 us
  Pallas kernels  35.8 us (90%)
  local copies, waits for them, and re-layouts  3.27 us (8%)
  between operations  0.65 us (2%)
    pallas_call x1, Pallas kernels, body(): pl.pallas_call(run, out_shape=(out, out), in_specs=[vmem] * 3, out_specs=...  35.8 us
    unnamed x8, local copies, waits for them, and re-layouts  3.27 us

profile of v1, /device:TPU:1, one launch (start us, length us, event | category | flops | bytes accessed | tf_op | source)
XLA Modules:
  0.0 39.7 jit_solution(15210069367514238980)
XLA Ops:
  0.6 0.0 copy-start
  0.6 0.7 %copy-done = f32[3,512]{1,0:T(4,128)S(1)} copy-done((f32[3,512]{1,0:T(4,128)S(1)}, f32[3,512]{1,0:T(4,128)}, u32[]{:S(2)}) %copy-start) | copy-done | bytes 6168
  1.3 0.0 copy-start.1
  1.3 0.7 %copy-done.1 = f32[3,512]{1,0:T(4,128)S(1)} copy-done((f32[3,512]{1,0:T(4,128)S(1)}, f32[3,512]{1,0:T(4,128)}, u32[]{:S(2)}) %copy-start.1) | copy-done | bytes 6168
  2.0 0.0 copy-start.2
  2.0 0.7 %copy-done.2 = f32[512]{0:T(512)S(1)} copy-done((f32[512]{0:T(512)S(1)}, f32[512]{0:T(512)}, u32[]{:S(2)}) %copy-start.2) | copy-done | bytes 2072
  2.7 35.8 %shard_map.50 = (f32[3,512]{1,0:T(4,128)S(1)}, f32[3,512]{1,0:T(4,128)S(1)}) custom-call(f32[3,512]{1,0:T(4,128)S(1)} %copy-done, f32[3,512]{1,0:T(4,128)S(1)} %copy-done.1, f32[1,512]{1,0:T(1,128)S(1)} %bitcast.1), custom_call_target="tpu_custom_call" | custom-call | tf_op jit(solution)/shard_map/pallas_call | solution.py:187
  38.5 0.6 %copy.7 = f32[3,512]{1,0:T(4,128)} copy(f32[3,512]{1,0:T(4,128)S(1)} %get-tuple-element.4) | data formatting | bytes 12288
  39.1 0.6 %copy.8 = f32[3,512]{1,0:T(4,128)} copy(f32[3,512]{1,0:T(4,128)S(1)} %get-tuple-element.5) | data formatting | bytes 12288
Async XLA Ops:
  0.6 0.7 %copy-start = (f32[3,512]{1,0:T(4,128)S(1)}, f32[3,512]{1,0:T(4,128)}, u32[]{:S(2)}) copy-start(f32[3,512]{1,0:T(4,128)} %refs_0_.1) | copy-start | bytes 18436
  1.3 0.7 %copy-start.1 = (f32[3,512]{1,0:T(4,128)S(1)}, f32[3,512]{1,0:T(4,128)}, u32[]{:S(2)}) copy-start(f32[3,512]{1,0:T(4,128)} %refs_1_.1) | copy-start | bytes 18436
  2.0 0.7 %copy-start.2 = (f32[512]{0:T(512)S(1)}, f32[512]{0:T(512)}, u32[]{:S(2)}) copy-start(f32[512]{0:T(512)} %param.5) | copy-start | bytes 6148
